TPU v7x, 32 devices: a whole 2x2x4 slice. The times are simulated.
32 devices in a mesh: ctx: 8 (over z, x), qg: 4 (over y, core).
Axes of the slice: x: 2, y: 2, z: 4, core: 2. Of those that a mesh axis runs over, the one named last changes fastest.
Arguments:
- queries: bfloat16 [16, 32, 768], P('qg'), may hold values from -9 to 9
- documents: bfloat16 [8, 4096, 768], P('qg', 'ctx'), may hold values from -2.5 to 2.5
- candidates: int32 [16, 4], replicated, may hold values from 0 to 7, all different within a row
Outputs:
- loss: float32 [], replicated
- grad_queries: bfloat16 [16, 32, 768], P('qg')
- grad_documents: bfloat16 [8, 4096, 768], P('qg', 'ctx')
Inputs may be any that keep to these rules, and one draw needn't show every extreme that they name: `candidates`: each row names 4 different documents; every document is named by some row.
All inputs are finite; a program needn't handle non-finite values.
Results may differ from a plain program's by a relative error of at most 0.006.
Values may be sent and summed in bfloat16 or wider, within the bound.
A program may use at most 64 MiB of HBM per device.

v0:
```python
import functools

import jax
import jax.numpy as jnp
from jax import lax
from jax.experimental import pallas as pl
from jax.experimental.pallas import tpu as pltpu
from jax.sharding import PartitionSpec as P

sharpness_factor = 2.0
loss_scale = 1024.0
MESH = pl.DeviceIdType.MESH
f32 = jnp.float32
bf16 = jnp.bfloat16


def each(lo, hi, f):
    if hi - lo <= 16:
        for k in range(lo, hi):
            f(k)
    else:
        pl.loop(lo, hi)(f)


def when(always, cond, f):
    if always:
        f()
    else:
        pl.when(cond)(f)


def wrap(i, n):
    return lax.rem(i + 2 * n, n)


def kernel(
    C, NQ, qlen,
    cand_hbm, q_hbm, d_hbm,
    loss_ref, gq_ref, gd,
    Q, D, E, G, M, L, Lr, T, S, Sh, Shr, Ss, SC, As, Ar, Bs, Br, Mine, Cs, Cr, Fs, Fr, cand,
    d_sem, ql, cand_sem, qs, qr, fs, ls, lr, ts, tr, sh_sem, a_s, a_r, b_s, b_r, c_s, c_r, f_s, f_r,
):
    nd, tok, width = D.shape
    rows = Q.shape[1]
    Y = NQ // 2
    nq = rows // qlen
    slots = cand.shape[0]
    NC = Mine.shape[0]
    cw = width // NC
    rpc = Cr.shape[2]
    half = rows // 2
    nred = half // rpc
    CZ = C // 2
    full = nred == CZ
    c = lax.axis_index("ctx")
    g = lax.axis_index("qg")
    m = c // 2
    b = lax.rem(c, 2)
    y = g // 2
    core = lax.rem(g, 2)
    sib = 2 * y + 1 - core

    def rc(src, dst, ssem, rsem, cc, gg):
        return pltpu.make_async_remote_copy(
            src_ref=src, dst_ref=dst, send_sem=ssem, recv_sem=rsem,
            device_id=(cc, gg), device_id_type=MESH,
        )

    barrier = pltpu.get_barrier_semaphore()
    for k in range(1, NQ):
        pl.semaphore_signal(barrier, inc=1, device_id=(c, wrap(g + k, NQ)), device_id_type=MESH)
    each(1, C, lambda k: pl.semaphore_signal(
        barrier, inc=1, device_id=(wrap(c + k, C), g), device_id_type=MESH))
    for k in range(1, Y):
        pl.semaphore_signal(
            barrier, inc=1, device_id=(2 * m + 1 - b, wrap(g + 2 * k, NQ)), device_id_type=MESH)
    q_own = pltpu.make_async_copy(q_hbm, Q.at[g], ql)
    q_own.start()
    cand_copy = pltpu.make_async_copy(cand_hbm, cand, cand_sem)
    cand_copy.start()
    dcopy = [pltpu.make_async_copy(d_hbm.at[d], D.at[d], d_sem.at[d]) for d in range(nd)]
    for x in dcopy:
        x.start()
    pl.semaphore_wait(barrier, NQ - 1 + C - 1 + Y - 1)

    def q_to_y(k):
        return rc(q_hbm, Q.at[g], qs.at[k], qr.at[g], c, wrap(g + 2 * k, NQ))

    q_to_sib = rc(q_hbm, Q.at[g], qs.at[0], qr.at[g], c, sib)
    for k in range(1, Y):
        q_to_y(k).start()
    q_to_sib.start()

    lane_q = lax.broadcasted_iota(jnp.int32, (NQ, rows), 1) // qlen
    sub_g = lax.broadcasted_iota(jnp.int32, (NQ, rows), 0)
    qid = sub_g * nq + lane_q
    ids = []
    cand_copy.wait()
    for k in range(slots):
        v = jnp.zeros((NQ, rows), jnp.int32)
        for q in range(cand.shape[1]):
            v = jnp.where(qid == q, cand[k, q], v)
        ids.append(v)

    def wait_q(src):
        rc(q_hbm, Q.at[src], qs.at[0], qr.at[src], c, sib).wait_recv()

    def fwd(first, n):
        qb = Q[pl.ds(first, n)].reshape(n * rows, width)
        for d in range(nd):
            lg = sharpness_factor * lax.dot_general(
                D[d], qb, (((1,), (1,)), ((), ())), preferred_element_type=f32)
            m = jnp.max(lg, axis=0, keepdims=True)
            e = jnp.exp(lg - m)
            lp = m + jnp.log(jnp.sum(e, axis=0, keepdims=True))
            for h in range(n):
                r = pl.ds(d * NQ + first + h, 1)
                E[first + h, d] = e[:, h * rows:(h + 1) * rows]
                M[r, :] = m[:, h * rows:(h + 1) * rows]
                L[r, :] = lp[:, h * rows:(h + 1) * rows]

    def a_copy(yb):
        return rc(As.at[yb], Ar.at[yb], a_s.at[yb], a_r.at[yb], c, sib)

    def gmat(yb):
        for d in range(nd):
            e = jnp.concatenate([E[2 * yb, d].astype(bf16), E[2 * yb + 1, d].astype(bf16)], axis=1)
            p = lax.dot_general(
                e, D[d], (((0,), (0,)), ((), ())), preferred_element_type=f32)
            G[d, pl.ds(2 * yb, 2)] = p.reshape(2, rows, width)
            As[yb, d] = G[d, 2 * yb + 1 - core].astype(bf16)
        a_copy(yb).start()

    q_own.wait()
    wait_q(sib)
    for x in dcopy:
        x.wait()
    fwd(2 * y, 2)
    gmat(y)
    fwd_copies = []
    for k in range(1, Y):
        src = wrap(g - 2 * k, NQ)
        wait_q(src)
        cp = rc(Q.at[src], Q.at[src], fs.at[k], qr.at[src], c, sib)
        cp.start()
        fwd_copies.append(cp)
        fwd(src, 1)
    for k in range(1, Y):
        src = wrap(sib - 2 * k, NQ)
        wait_q(src)
        fwd(src, 1)

    def l_copy(k):
        return rc(L, Lr.at[k], ls.at[k], lr.at[k], wrap(c + k, C), g)

    each(1, C, lambda k: l_copy(k).start())
    for k in range(1, Y):
        gmat(wrap(y - k, Y))
    Lr[0] = L[...]
    each(1, C, lambda k: l_copy(k).wait_recv())
    parts = Lr[...]
    top = jnp.max(parts, axis=0)
    lse = top + jnp.log(jnp.sum(jnp.exp(parts - top[None]), axis=0))

    same = (lax.broadcasted_iota(jnp.int32, (rows, rows), 0) // qlen
            == lax.broadcasted_iota(jnp.int32, (rows, rows), 1) // qlen).astype(f32)
    T[g] = lax.dot_general(
        lse, same, (((1,), (0,)), ((), ())),
        precision=lax.Precision.HIGHEST, preferred_element_type=f32) / sharpness_factor

    def t_copy(k):
        return rc(T.at[g], T.at[g], ts.at[k], tr.at[k], c, wrap(g + k, NQ))

    for k in range(1, NQ):
        t_copy(k).start()
    Sh[...] = jnp.exp(M[...] - lse)
    sh_copy = rc(Sh, Shr, sh_sem.at[0], sh_sem.at[1], c, sib)
    sh_copy.start()
    for k in range(1, NQ):
        src = wrap(g - k, NQ)
        rc(T.at[src], T.at[src], ts.at[k], tr.at[k], c, src).wait_recv()

    pairs = []
    for k in range(slots):
        v = jnp.zeros((NQ, rows), f32)
        for gg in range(NQ):
            for d in range(nd):
                v = jnp.where(ids[k] == gg * nd + d, T[gg, d * NQ:(d + 1) * NQ, :], v)
        pairs.append(v)
    highest = functools.reduce(jnp.maximum, pairs)
    total = highest + jnp.log(functools.reduce(jnp.add, [jnp.exp(p - highest) for p in pairs]))
    loss_ref[0, 0] = jnp.sum(total - pairs[0]) / (NQ * rows)
    dz = [
        loss_scale / (NQ * nq) * (jnp.exp(p - total) - (1.0 if k == 0 else 0.0))
        for k, p in enumerate(pairs)
    ]
    sh_copy.wait_recv()
    for d in range(nd):
        r = slice(d * NQ, (d + 1) * NQ)
        for grp, shrink, dst in ((g, Sh, S), (sib, Shr, Ss)):
            w = jnp.zeros((NQ, rows), f32)
            for k in range(slots):
                w = w + jnp.where(ids[k] == grp * nd + d, dz[k], 0.0)
            dst[r, :] = w * shrink[r, :]
    own = [
        src[pl.ds(d * NQ + 2 * yy + core, 1), :]
        for yy in range(Y) for src in (S, Ss) for d in range(nd)
    ]
    St = jnp.transpose(jnp.concatenate(own, axis=0))
    for i in range(len(own)):
        SC[i // (2 * nd), i % (2 * nd)] = jnp.broadcast_to(St[:, i:i + 1], (rows, 128))

    for k in range(Y):
        a_copy(wrap(y - k, Y)).wait_recv()

    def scaled(yy, h, lo):
        at = slice(lo, lo + 128)
        r = pl.ds(pl.multiple_of(h * half, half), half)
        v = SC[yy, 0, r, :] * G[0, 2 * yy + core, r, at]
        for d in range(1, nd):
            v = v + SC[yy, d, r, :] * G[d, 2 * yy + core, r, at]
        for d in range(nd):
            v = v + SC[yy, nd + d, r, :] * Ar[yy, d, r, at].astype(f32)
        return v

    u = 2 * y + b

    def b_copy(n, k):
        to = wrap(u + k, 2 * Y)
        return to, rc(Bs.at[n, k], Br.at[n, k], b_s.at[n, k], b_r.at[n, k],
                      2 * m + lax.rem(to, 2), 2 * (to // 2) + core)

    for n in range(NC):
        for k in range(1, 2 * Y):
            to, cp = b_copy(n, k)
            for lo in range(0, cw, 128):
                Bs[n, k, :, lo:lo + 128] = scaled(
                    to // 2, lax.rem(to, 2), n * cw + lo).astype(bf16)
            cp.start()
    for n in range(NC):
        for lo in range(0, cw, 128):
            Mine[n, :, lo:lo + 128] = scaled(y, b, n * cw + lo)

    def doc_grad(d):
        acc = None
        for yb in range(Y):
            r = d * NQ + 2 * yb
            wt = jnp.concatenate(
                [(E[2 * yb + h, d] * S[r + h:r + h + 1, :]).astype(bf16) for h in range(2)], axis=1)
            part = jnp.dot(wt, Q[2 * yb:2 * yb + 2].reshape(2 * rows, width),
                           preferred_element_type=f32)
            acc = part if acc is None else acc + part
        gd[d] = acc.astype(bf16)

    for d in range(nd // 2):
        doc_grad(d)

    share = lax.rem(m, nred)

    def c_copy(n, k):
        to = wrap(m + k, CZ)
        return to, rc(
            Cs.at[n, lax.rem(to, nred)], Cr.at[n, k], c_s.at[n, k], c_r.at[n, k], 2 * to + b, g)

    def f_copy(n, k):
        return rc(Fs.at[n], Fr.at[n, b, share], f_s.at[n, k], f_r.at[n, k], wrap(c + k, C), g)

    for n in range(NC):
        for k in range(1, 2 * Y):
            b_copy(n, k)[1].wait_recv()
            Mine[n] = Mine[n] + Br[n, k].astype(f32)
        Cs[n] = Mine[n].astype(bf16).reshape(nred, rpc, cw)

        def c_start(k, n=n):
            to, cp = c_copy(n, k)
            when(full, to < nred, cp.start)

        each(1, CZ, c_start)

    for d in range(nd // 2, nd):
        doc_grad(d)

    for n in range(NC):
        def reduce_share(n=n):
            at = pl.multiple_of(share * rpc, rpc)
            Cr[n, 0] = jnp.zeros((rpc, cw), bf16)
            each(1, CZ, lambda k: c_copy(n, k)[1].wait_recv())
            v = Mine[n, pl.ds(at, rpc), :] + jnp.sum(Cr[n].astype(f32), axis=0)
            Fs[n] = v.astype(bf16)
            each(1, C, lambda k: f_copy(n, k).start())
            Fr[n, b, share] = Fs[n]

        when(full, m < nred, reduce_share)

    for n in range(NC):
        def f_wait(k, n=n):
            src = wrap(c - k, C)
            cp = rc(Fs.at[n], Fr.at[n, lax.rem(src, 2), lax.rem(src // 2, nred)],
                    f_s.at[n, k], f_r.at[n, k], src, g)
            when(full, src // 2 < nred, cp.wait_recv)

        each(1, C, f_wait)
        gq_ref[:, n * cw:(n + 1) * cw] = Fr[n].reshape(rows, cw)

    for k in range(1, Y):
        q_to_y(k).wait_send()
    q_to_sib.wait_send()
    for cp in fwd_copies:
        cp.wait_send()
    each(1, C, lambda k: l_copy(k).wait_send())
    for k in range(1, NQ):
        t_copy(k).wait_send()
    sh_copy.wait_send()
    for yy in range(Y):
        a_copy(yy).wait_send()
    for n in range(NC):
        for k in range(1, 2 * Y):
            b_copy(n, k)[1].wait_send()

        def c_done(k, n=n):
            to, cp = c_copy(n, k)
            when(full, to < nred, cp.wait_send)

        each(1, CZ, c_done)
        when(full, m < nred, lambda n=n: each(1, C, lambda k: f_copy(n, k).wait_send()))


def write_out(gq_in, gd_in, gq_out, gd_out, gq_sem, gd_sem):
    a = pltpu.make_async_copy(gd_in, gd_out, gd_sem)
    b = pltpu.make_async_copy(gq_in, gq_out, gq_sem)
    a.start()
    b.start()
    a.wait()
    b.wait()


def per_device(C, NQ, queries, documents, candidates):
    nq, qlen, width = queries.shape
    nd, tok, _ = documents.shape
    rows = nq * qlen
    Y = NQ // 2
    half = rows // 2
    rpc = max(16, rows // C)
    nred = half // rpc
    CZ = C // 2
    NC = 3 if width % 384 == 0 else 1
    cw = width // NC
    dma = pltpu.SemaphoreType.DMA
    V = pltpu.VMEM
    loss, gq, gd = pl.pallas_call(
        functools.partial(kernel, C, NQ, qlen),
        out_shape=(
            jax.ShapeDtypeStruct((1, 1), f32),
            pltpu.VMEM((rows, width), bf16),
            pltpu.VMEM((nd, tok, width), bf16),
        ),
        in_specs=[
            pl.BlockSpec(memory_space=pltpu.HBM),
            pl.BlockSpec(memory_space=pltpu.HBM),
            pl.BlockSpec(memory_space=pltpu.HBM),
        ],
        out_specs=(
            pl.BlockSpec(memory_space=pltpu.SMEM),
            pl.BlockSpec(memory_space=pltpu.VMEM),
            pl.BlockSpec(memory_space=pltpu.VMEM),
        ),
        scratch_shapes=[
            V((NQ, rows, width), bf16),
            V((nd, tok, width), bf16),
            V((NQ, nd, tok, rows), f32),
            V((nd, NQ, rows, width), f32),
            V((nd * NQ, rows), f32),
            V((nd * NQ, rows), f32),
            V((C, nd * NQ, rows), f32),
            V((NQ, nd * NQ, rows), f32),
            V((nd * NQ, rows), f32),
            V((nd * NQ, rows), f32),
            V((nd * NQ, rows), f32),
            V((nd * NQ, rows), f32),
            V((Y, 2 * nd, rows, 128), f32),
            V((Y, nd, rows, width), bf16),
            V((Y, nd, rows, width), bf16),
            V((NC, 2 * Y, half, cw), bf16),
            V((NC, 2 * Y, half, cw), bf16),
            V((NC, half, cw), f32),
            V((NC, nred, rpc, cw), bf16),
            V((NC, CZ, rpc, cw), bf16),
            V((NC, rpc, cw), bf16),
            V((NC, 2, nred, rpc, cw), bf16),
            pltpu.SMEM(candidates.shape[::-1], jnp.int32),
            dma((nd,)), dma, dma,
            dma((Y,)), dma((NQ,)), dma((Y,)),
            dma((C,)), dma((C,)),
            dma((NQ,)), dma((NQ,)), dma((2,)),
            dma((Y,)), dma((Y,)),
            dma((NC, 2 * Y)), dma((NC, 2 * Y)),
            dma((NC, CZ)), dma((NC, CZ)),
            dma((NC, C)), dma((NC, C)),
        ],
        compiler_params=pltpu.CompilerParams(
            collective_id=0, has_side_effects=True, vmem_limit_bytes=48 * 1024 * 1024),
    )(
        pltpu.with_memory_space_constraint(jnp.transpose(candidates), pltpu.HBM),
        pltpu.with_memory_space_constraint(queries.reshape(rows, width), pltpu.HBM),
        pltpu.with_memory_space_constraint(documents, pltpu.HBM),
    )
    gq, gd = pl.pallas_call(
        write_out,
        out_shape=(
            jax.ShapeDtypeStruct((rows, width), bf16),
            jax.ShapeDtypeStruct((nd, tok, width), bf16),
        ),
        in_specs=[pl.BlockSpec(memory_space=pl.ANY)] * 2,
        out_specs=(pl.BlockSpec(memory_space=pl.ANY),) * 2,
        scratch_shapes=[dma, dma],
    )(
        pltpu.with_memory_space_constraint(gq, pltpu.VMEM),
        pltpu.with_memory_space_constraint(gd, pltpu.VMEM),
    )
    return loss.reshape(()), gq.reshape(nq, qlen, width), gd


def solution(mesh):
    return jax.shard_map(
        functools.partial(per_device, mesh.shape["ctx"], mesh.shape["qg"]),
        mesh=mesh,
        in_specs=(P("qg", None, None), P("qg", "ctx", None), P()),
        out_specs=(P(), P("qg", None, None), P("qg", "ctx", None)),
        check_vma=False,
    )
```

profile of v0, /device:TPU:0, one launch (start us, length us, event | category | flops | bytes accessed | tf_op | source)
XLA Modules:
  0.0 40.1 jit_solution(9836806651441008851)
XLA Ops:
  0.6 36.5 %shard_map.58 = (f32[1,1]{1,0:T(1,128)}, bf16[128,768]{1,0:T(8,128)(2,1)S(1)}, bf16[2,512,768]{2,1,0:T(8,128)(2,1)S(1)}) custom-call(s32[4,16]{1,0:T(4,128)} %bitcast.5, bf16[128,768]{1,0:T(8,128)(2,1)} %bitcast.4, bf16[2,512,768]{2,1,0:T(8,128)(2,1)} %d_hbm.1), custom_call_target="tpu_custom_call" | custom-call | tf_op jit(solution)/shard_map/pallas_call | solution.py:350
  37.1 1.2 %shard_map.59 = (bf16[128,768]{1,0:T(8,128)(2,1)}, bf16[2,512,768]{2,1,0:T(8,128)(2,1)}) custom-call(bf16[128,768]{1,0:T(8,128)(2,1)S(1)} %get-tuple-element.9.gq_in, bf16[2,512,768]{2,1,0:T(8,128)(2,1)S(1)} %get-tuple-element.10.gd_in), custom_call_target="tpu_custom_call" | custom-call | tf_op jit(solution)/shard_map/pallas_call | solution.py:407
where the time goes:
time: 40.3 us; the launch traced here: 40.1 us
  Pallas kernels  37.7 us (94%)
  between operations  2.4 us (6%)
    pallas_call x1, Pallas kernels, per_device(): pl.pallas_call(functools.partial(kernel, C, NQ, qlen), out_shape=(jax.Sha...  36.5 us
    pallas_call x1, Pallas kernels, per_device(): pl.pallas_call(write_out, out_shape=(jax.ShapeDtypeStruct((rows, width),...  1.21 us

commit v1 on v0

--- a/solution.py
+++ b/solution.py
@@ -122,21 +122,22 @@
     def a_copy(yb):
         return rc(As.at[yb], Ar.at[yb], a_s.at[yb], a_r.at[yb], c, sib)
 
-    def gmat(yb):
-        for d in range(nd):
+    def gmat(yb, docs, last):
+        for d in docs:
             e = jnp.concatenate([E[2 * yb, d].astype(bf16), E[2 * yb + 1, d].astype(bf16)], axis=1)
             p = lax.dot_general(
                 e, D[d], (((0,), (0,)), ((), ())), preferred_element_type=f32)
             G[d, pl.ds(2 * yb, 2)] = p.reshape(2, rows, width)
             As[yb, d] = G[d, 2 * yb + 1 - core].astype(bf16)
-        a_copy(yb).start()
+        if last:
+            a_copy(yb).start()
 
     q_own.wait()
     wait_q(sib)
     for x in dcopy:
         x.wait()
     fwd(2 * y, 2)
-    gmat(y)
+    gmat(y, range(nd // 2), False)
     fwd_copies = []
     for k in range(1, Y):
         src = wrap(g - 2 * k, NQ)
@@ -145,6 +146,7 @@
         cp.start()
         fwd_copies.append(cp)
         fwd(src, 1)
+    gmat(y, range(nd // 2, nd), True)
     for k in range(1, Y):
         src = wrap(sib - 2 * k, NQ)
         wait_q(src)
@@ -155,7 +157,7 @@
 
     each(1, C, lambda k: l_copy(k).start())
     for k in range(1, Y):
-        gmat(wrap(y - k, Y))
+        gmat(wrap(y - k, Y), range(nd), True)
     Lr[0] = L[...]
     each(1, C, lambda k: l_copy(k).wait_recv())
     parts = Lr[...]
@@ -343,7 +345,7 @@
     rpc = max(16, rows // C)
     nred = half // rpc
     CZ = C // 2
-    NC = 3 if width % 384 == 0 else 1
+    NC = 6 if width % 768 == 0 else 1
     cw = width // NC
     dma = pltpu.SemaphoreType.DMA
     V = pltpu.VMEM

time: 40.3 us -> 41.7 us (1.035)
  Pallas kernels: 37.7 us -> 39.1 us
    pallas_call x1, Pallas kernels: 36.5 us -> 37.9 us  [per_device(): pl.pallas_call(functools.partial(kernel, C, NQ, qlen), out_shape=(jax.Sha...]
where the time goes in v1:
time: 41.7 us; the launch traced here: 41.5 us
  Pallas kernels  39.1 us (94%)
  between operations  2.4 us (6%)
    pallas_call x1, Pallas kernels, per_device(): pl.pallas_call(functools.partial(kernel, C, NQ, qlen), out_shape=(jax.Sha...  37.9 us
    pallas_call x1, Pallas kernels, per_device(): pl.pallas_call(write_out, out_shape=(jax.ShapeDtypeStruct((rows, width),...  1.21 us

profile of v1, /device:TPU:0, one launch (start us, length us, event | category | flops | bytes accessed | tf_op | source)
XLA Modules:
  0.0 41.5 jit_solution(14260153302166434171)
XLA Ops:
  0.6 37.9 %shard_map.58 = (f32[1,1]{1,0:T(1,128)}, bf16[128,768]{1,0:T(8,128)(2,1)S(1)}, bf16[2,512,768]{2,1,0:T(8,128)(2,1)S(1)}) custom-call(s32[4,16]{1,0:T(4,128)} %bitcast.5, bf16[128,768]{1,0:T(8,128)(2,1)} %bitcast.4, bf16[2,512,768]{2,1,0:T(8,128)(2,1)} %d_hbm.1), custom_call_target="tpu_custom_call" | custom-call | tf_op jit(solution)/shard_map/pallas_call | solution.py:352
  38.5 1.2 %shard_map.59 = (bf16[128,768]{1,0:T(8,128)(2,1)}, bf16[2,512,768]{2,1,0:T(8,128)(2,1)}) custom-call(bf16[128,768]{1,0:T(8,128)(2,1)S(1)} %get-tuple-element.9.gq_in, bf16[2,512,768]{2,1,0:T(8,128)(2,1)S(1)} %get-tuple-element.10.gd_in), custom_call_target="tpu_custom_call" | custom-call | tf_op jit(solution)/shard_map/pallas_call | solution.py:409

commit v2 on v0

--- a/solution.py
+++ b/solution.py
@@ -343,7 +343,7 @@
     rpc = max(16, rows // C)
     nred = half // rpc
     CZ = C // 2
-    NC = 3 if width % 384 == 0 else 1
+    NC = 2 if width % 256 == 0 else 1
     cw = width // NC
     dma = pltpu.SemaphoreType.DMA
     V = pltpu.VMEM

time: 40.3 us -> 40.5 us (level)
  no operation moved by 1% of the time
where the time goes in v2:
time: 40.5 us; the launch traced here: 40.4 us
  Pallas kernels  38 us (94%)
  between operations  2.4 us (6%)
    pallas_call x1, Pallas kernels, per_device(): pl.pallas_call(functools.partial(kernel, C, NQ, qlen), out_shape=(jax.Sha...  36.8 us
    pallas_call x1, Pallas kernels, per_device(): pl.pallas_call(write_out, out_shape=(jax.ShapeDtypeStruct((rows, width),...  1.21 us

profile of v2, /device:TPU:0, one launch (start us, length us, event | category | flops | bytes accessed | tf_op | source)
XLA Modules:
  0.0 40.4 jit_solution(168111984976713177)
XLA Ops:
  0.6 36.8 %shard_map.58 = (f32[1,1]{1,0:T(1,128)}, bf16[128,768]{1,0:T(8,128)(2,1)S(1)}, bf16[2,512,768]{2,1,0:T(8,128)(2,1)S(1)}) custom-call(s32[4,16]{1,0:T(4,128)} %bitcast.5, bf16[128,768]{1,0:T(8,128)(2,1)} %bitcast.4, bf16[2,512,768]{2,1,0:T(8,128)(2,1)} %d_hbm.1), custom_call_target="tpu_custom_call" | custom-call | tf_op jit(solution)/shard_map/pallas_call | solution.py:350
  37.4 1.2 %shard_map.59 = (bf16[128,768]{1,0:T(8,128)(2,1)}, bf16[2,512,768]{2,1,0:T(8,128)(2,1)}) custom-call(bf16[128,768]{1,0:T(8,128)(2,1)S(1)} %get-tuple-element.9.gq_in, bf16[2,512,768]{2,1,0:T(8,128)(2,1)S(1)} %get-tuple-element.10.gd_in), custom_call_target="tpu_custom_call" | custom-call | tf_op jit(solution)/shard_map/pallas_call | solution.py:407
